TPU v7x, 512 devices: a whole 4x8x8 slice. The times are simulated.
512 devices in a mesh: row: 16 (over y, core), ma: 32 (over x, z).
Axes of the slice: x: 4, y: 8, z: 8, core: 2. Of those that a mesh axis runs over, the one named last changes fastest.
Arguments:
- field_a: float32 [256, 2, 128, 384], P('row', None, 'ma'), may hold values from -6 to 6
- field_b: float32 [256, 2, 128, 384], P('row', None, 'ma'), may hold values from -6 to 6
- mode_ids: int32 [128], replicated, may hold values from 0 to 383, as said below
- legendre: bfloat16 [128, 384, 384], P('ma'), may hold values from -0.3125 to 0.3125
- quad_weights: float32 [384], replicated, may hold values from 0.4 to 1.2
- colat_cos: float32 [384], replicated, may hold values from -1 to 1
- lorentz: float32 [256, 384], P('row'), may hold values from 0.2 to 2
- theta_order: int32 [384], replicated, may hold values from 0 to 383, each once
- inverse: bfloat16 [384, 256, 256], P('row'), may hold values from -1 to 1
Outputs:
- new_a: float32 [256, 2, 128, 384], P('row', None, 'ma')
- new_b: float32 [256, 2, 128, 384], P('row', None, 'ma')
- zonal_mean: float32 [256, 384], P('row', 'ma')
Inputs may be any that keep to these rules, and one draw needn't show every extreme that they name: `mode_ids`: for each k, entries 2k and 2k+1 are a mode m below 192 and its partner 384 - 1 - m; all entries differ; some pair holds mode 0. `theta_order`: every row index appears once.
All inputs are finite; a program needn't handle non-finite values.
Results may differ from a plain program's by a relative error of at most 0.03.
Values may be sent and summed in bfloat16 or wider, within the bound.
A program may use at most 128 MiB of HBM per device.

v0:
```python
import math

import jax
import jax.numpy as jnp
from jax import lax
from jax.experimental import pallas as pl
from jax.experimental.pallas import tpu as pltpu
from jax.sharding import PartitionSpec as P

STEPS = 3
NPHI = 768
N = 384
NMA = 32
NROW = 16
F32 = jnp.float32
BF16 = jnp.bfloat16
MESH = pl.DeviceIdType.MESH


def iota(shape, dim):
    return lax.broadcasted_iota(jnp.int32, shape, dim)


def dot(a, b):
    return jnp.dot(a, b, preferred_element_type=F32)


def onehot(test):
    return jnp.where(test, 1.0, 0.0).astype(BF16)


def exact_dot(a, hot):
    hi = a.astype(BF16)
    rest = a - hi.astype(F32)
    mid = rest.astype(BF16)
    low = (rest - mid.astype(F32)).astype(BF16)
    return dot(hi, hot) + dot(mid, hot) + dot(low, hot)


def kernel(
    fa, fb, ids_s, theta_s, ids_v, theta_v, leg, qw, colat, lor, inv_hbm,
    out_a, out_b, out_z,
    legp, wp, spec, xs, tt, bt, val, k1, k2, force, yf, gs, g, ms, h, rs, c, us, s, inv, bf,
    send_sem, recv_sem, inv_sem,
):
    row = lax.axis_index("row")
    ma = lax.axis_index("ma")

    barrier = pltpu.get_barrier_semaphore()

    def greet_ma(i, _):
        pl.semaphore_signal(barrier, inc=1, device_id={"ma": lax.rem(ma + i, NMA)}, device_id_type=MESH)
        return 0

    def greet_row(i, _):
        pl.semaphore_signal(barrier, inc=1, device_id={"row": lax.rem(row + i, NROW)}, device_id_type=MESH)
        return 0

    lax.fori_loop(1, NMA, greet_ma, 0)
    lax.fori_loop(1, NROW, greet_row, 0)
    inv_copy = pltpu.make_async_copy(inv_hbm, inv, inv_sem)
    inv_copy.start()

    lane = iota((1, N), 1)
    lane128 = iota((1, 128), 1)
    degree = (lane & 15) * 24 + (lane >> 4)

    def live(m):
        return degree >= ids_s[ma * 4 + m]

    to_degree = onehot(iota((N, N), 0) == degree)
    nat = onehot(iota((N, N), 0) == theta_v[...])
    shuffle = onehot(iota((N, N), 0) == (lane & 31) * 12 + (lane >> 5))
    pick = jnp.transpose(dot(nat, shuffle)).astype(BF16)
    for m in range(4):
        legp[m] = dot(pick, dot(leg[m], to_degree).astype(BF16)).astype(BF16)

    for m in range(4):
        for part in range(2):
            for f, field in ((0, fa), (1, fb)):
                piece = field[:, part, m, :]
                hi = piece.astype(BF16)
                lo = (piece - hi.astype(F32)).astype(BF16)
                moved = jnp.where(live(m), dot(hi, to_degree) + dot(lo, to_degree), 0.0)
                spec[m * 4 + part * 2 + f] = moved
                xs[m * 4 + part * 2 + f] = moved.astype(BF16)

    pl.semaphore_wait(barrier, NMA + NROW - 2)

    def send(src, dst, count, axis, me, k):
        def one(i, _):
            to = lax.rem(me + i, count)
            pltpu.make_async_remote_copy(
                src_ref=src.at[to],
                dst_ref=dst.at[me],
                send_sem=send_sem.at[k],
                recv_sem=recv_sem.at[k],
                device_id={axis: to},
                device_id_type=MESH,
            ).start()
            return 0

        lax.fori_loop(1, count, one, 0)
        dst[me] = src[me]

    def arrive(src, dst, count, k):
        pltpu.make_async_copy(dst.at[pl.ds(0, count - 1)], dst.at[pl.ds(0, count - 1)], recv_sem.at[k]).wait()
        pltpu.make_async_copy(src.at[pl.ds(0, count - 1)], src.at[pl.ds(0, count - 1)], send_sem.at[k]).wait()

    def swap16(load, store):
        for q in range(3):
            cols = slice(q * 128, q * 128 + 128)
            parts = [load(i, cols) for i in range(16)]
            for k in (1, 2, 4, 8):
                low = (lane128 & k) == 0
                for i in range(16):
                    if i & k == 0:
                        a, b = parts[i], parts[i + k]
                        parts[i] = jnp.where(low, a, pltpu.roll(b, k, 1))
                        parts[i + k] = jnp.where(low, pltpu.roll(a, 128 - k, 1), b)
            for i in range(16):
                store(i, cols, parts[i])

    def prepare_longitude():
        n = iota((1, 256), 1)
        expand = onehot(iota((128, 256), 0) == (n >> 3) * 4 + (n & 3))
        ids = jnp.broadcast_to(ids_v[...], (8, 128))
        top = ids >> 4
        mode = 16.0 * dot(top.astype(F32).astype(BF16), expand) + dot((ids & 15).astype(F32).astype(BF16), expand)
        mode = mode[0:1]

        def angles(count, period):
            k = mode * iota((count, 256), 0).astype(F32)
            k = k - period * jnp.floor((k + 0.5) * (1.0 / period))
            k = jnp.where(k > period / 2, k - period, k)
            return k * (2.0 * math.pi / period)

        coarse = angles(24, 24)
        fine = angles(32, NPHI)
        cos_c, sin_c = jnp.cos(coarse), jnp.sin(coarse)
        cos_f, sin_f = jnp.cos(fine), jnp.sin(fine)
        is_cos = (n & 4) == 0
        lead_c = jnp.where(is_cos, cos_c, -sin_c)
        lead_s = jnp.where(is_cos, sin_c, cos_c)
        for a in range(24):
            value = lead_c[a:a + 1] * cos_f - lead_s[a:a + 1] * sin_f
            val[a * 32:a * 32 + 32, :] = value
            tt[a * 32:a * 32 + 32, :] = (value * (1.0 / math.sqrt(128))).astype(BF16)
        for a in range(3):
            bt[:, a * 256:a * 256 + 256] = (
                jnp.transpose(val[a * 256:a * 256 + 256, :]) * math.sqrt(2.0 / NPHI)
            ).astype(BF16)

        own = jnp.zeros((1, N), jnp.int32)
        for t in range(12):
            own = jnp.where((lane >> 5) == t, theta_s[ma * 12 + t], own)
        hot = onehot(iota((N, N), 0) == own)
        is_a = (lane & 16) == 0
        cosines = exact_dot(jnp.broadcast_to(colat[...], (8, N)), hot)[0:1]
        k1[...] = jnp.where(is_a, 2.0 * cosines, -2.0 * cosines)
        energy = exact_dot(lor[...], hot)
        energy = jnp.sum(jnp.where(iota((16, N), 0) == (lane & 15), energy, 0.0), axis=0, keepdims=True)
        k2[...] = jnp.where(is_a, energy, 1.0)

    def prepare_weighted():
        column = jnp.transpose(jnp.broadcast_to(qw[...], (128, N)))[:, 0:1]
        for m in range(4):
            w = (column * leg[m].astype(F32)).astype(BF16)
            w = dot(pick_ref[...], dot(w, to_degree).astype(BF16))
            wp[m] = jnp.where(live(m), w, 0.0).astype(BF16)

    pick_ref = bf.at[0:N, :]
    pick_ref[...] = pick

    def step(n, _):
        for m in range(4):
            x0 = xs[m * 4:m * 4 + 2].reshape(32, N)
            x1 = xs[m * 4 + 2:m * 4 + 4].reshape(32, N)
            x = jnp.concatenate([x0] * 4 + [x1] * 4, axis=0)
            y = lax.dot_general(legp[m], x, (((1,), (1,)), ((), ())), preferred_element_type=F32)
            for part in range(2):
                for q in range(3):
                    pieces = [
                        y[(4 * q + j) * 32:(4 * q + j) * 32 + 32, part * 128:part * 128 + 128] for j in range(4)
                    ]
                    piece = pieces[0]
                    for j in range(1, 4):
                        piece = jnp.where((lane128 >> 5) == j, pieces[j], piece)
                    yf[q, pl.ds(part * 4 + m, 32, stride=8), :] = piece
        for q in range(3):
            gs[:, :, q * 128:q * 128 + 128] = yf[q].reshape(NMA, 8, 128).astype(BF16)
        send(gs, g, NMA, "ma", ma, 0)
        pl.when(n == 0)(prepare_longitude)
        arrive(gs, g, NMA, 0)

        grid = g[...].astype(F32).reshape(256, N)
        swapped = []
        for q in range(3):
            piece = grid[:, q * 128:q * 128 + 128]
            swapped.append(
                jnp.where((lane128 & 16) == 0, pltpu.roll(piece, 112, 1), pltpu.roll(piece, 16, 1))
            )
        both = jnp.concatenate([grid] + swapped, axis=1).astype(BF16)
        total = jnp.zeros((1, N), F32)
        for a in range(3):
            phys = dot(tt[a * 256:a * 256 + 256, :], both)
            value = phys[:, N:] * (k1[...] + k2[...] * phys[:, :N])
            force[a * 256:a * 256 + 256, :] = value.astype(BF16)
            total = total + jnp.sum(value, axis=0, keepdims=True)
        out_z[...] = jnp.broadcast_to(total * (1.0 / NPHI), (8, N))
        ms[...] = dot(bt[...], force[...]).reshape(NMA, 8, N).astype(BF16)
        send(ms, h, NMA, "ma", ma, 1)
        pl.when(n == 0)(prepare_weighted)
        arrive(ms, h, NMA, 1)

        for q in range(3):
            yf[q] = h[:, :, q * 128:q * 128 + 128].astype(F32).reshape(256, 128)
        for m in range(4):
            pieces = []
            for t in range(12):
                q, j = t // 4, t % 4
                p0 = yf[q, pl.ds(m, 32, stride=8), :]
                p1 = yf[q, pl.ds(4 + m, 32, stride=8), :]
                if j != 0:
                    p0 = pltpu.roll(p0, 128 - 32 * j, 1)
                if j != 1:
                    p1 = pltpu.roll(p1, (160 - 32 * j) % 128, 1)
                pieces.append(jnp.where(lane128 < 32, p0, p1))
            z = jnp.transpose(jnp.concatenate(pieces, axis=0))[0:64].astype(BF16)
            term = (0.25 * dot(z, wp[m])).astype(BF16).astype(F32)
            val_rows = spec[m * 4:m * 4 + 4].reshape(64, N) + term
            spec[m * 4:m * 4 + 4] = val_rows.astype(BF16).astype(F32).reshape(4, 16, N)

        def put_rs(i, cols, v):
            rs[i, :, cols] = v.astype(BF16)

        swap16(lambda i, cols: spec[i, :, cols], put_rs)
        send(rs, c, NROW, "row", row, 2)
        pl.when(n == 0)(inv_copy.wait)
        arrive(rs, c, NROW, 2)

        for q in range(3):
            right = c[:, :, q * 128:q * 128 + 128].reshape(256, 128)
            solved = dot(inv[q * 8], right)
            for i in range(1, 8):
                solved = jnp.where((lane128 >> 4) == i, dot(inv[q * 8 + i], right), solved)
            us[:, :, q * 128:q * 128 + 128] = solved.astype(BF16).reshape(NROW, 16, 128)
        send(us, s, NROW, "row", row, 3)
        arrive(us, s, NROW, 3)

        def put_spec(i, cols, v):
            spec[i, :, cols] = v
            xs[i, :, cols] = v.astype(BF16)

        swap16(lambda i, cols: s[i, :, cols].astype(F32), put_spec)
        return 0

    lax.fori_loop(0, STEPS, step, 0)

    from_degree = onehot((iota((N, N), 0) & 15) * 24 + (iota((N, N), 0) >> 4) == iota((N, N), 1))
    result = dot(xs[...].reshape(256, N), from_degree)
    for m in range(4):
        for part in range(2):
            for f, out in ((0, out_a), (1, out_b)):
                i = m * 4 + part * 2 + f
                for q in range(3):
                    out[q, pl.ds(part * 4 + m, 16, stride=8), :] = result[i * 16:i * 16 + 16, q * 128:q * 128 + 128]


def shards(
    field_a, field_b, mode_ids, legendre, quad_weights, colat_cos, lorentz, theta_order, inverse
):
    vmem = pl.BlockSpec(memory_space=pltpu.VMEM)
    smem = pl.BlockSpec(memory_space=pltpu.SMEM)
    out_a, out_b, out_z = pl.pallas_call(
        kernel,
        out_shape=(
            jax.ShapeDtypeStruct((3, 128, 128), F32),
            jax.ShapeDtypeStruct((3, 128, 128), F32),
            jax.ShapeDtypeStruct((8, N), F32),
        ),
        in_specs=[vmem, vmem, smem, smem, vmem, vmem, vmem, vmem, vmem, vmem, pl.BlockSpec(memory_space=pl.ANY)],
        out_specs=(vmem, vmem, vmem),
        scratch_shapes=[
            pltpu.VMEM((4, N, N), BF16),
            pltpu.VMEM((4, N, N), BF16),
            pltpu.VMEM((16, 16, N), F32),
            pltpu.VMEM((16, 16, N), BF16),
            pltpu.VMEM((NPHI, 256), BF16),
            pltpu.VMEM((256, NPHI), BF16),
            pltpu.VMEM((NPHI, 256), F32),
            pltpu.VMEM((1, N), F32),
            pltpu.VMEM((1, N), F32),
            pltpu.VMEM((NPHI, N), BF16),
            pltpu.VMEM((3, 256, 128), F32),
            pltpu.VMEM((NMA, 8, N), BF16),
            pltpu.VMEM((NMA, 8, N), BF16),
            pltpu.VMEM((NMA, 8, N), BF16),
            pltpu.VMEM((NMA, 8, N), BF16),
            pltpu.VMEM((NROW, 16, N), BF16),
            pltpu.VMEM((NROW, 16, N), BF16),
            pltpu.VMEM((NROW, 16, N), BF16),
            pltpu.VMEM((NROW, 16, N), BF16),
            pltpu.VMEM((24, 256, 256), BF16),
            pltpu.VMEM((N, N), BF16),
            pltpu.SemaphoreType.DMA((4,)),
            pltpu.SemaphoreType.DMA((4,)),
            pltpu.SemaphoreType.DMA,
        ],
        compiler_params=pltpu.CompilerParams(
            collective_id=0, has_side_effects=True, vmem_limit_bytes=48 * 1024 * 1024
        ),
        name="shell_steps",
    )(
        field_a, field_b, mode_ids, theta_order, mode_ids.reshape(1, 128), theta_order.reshape(1, N),
        legendre, quad_weights.reshape(1, N), colat_cos.reshape(1, N), lorentz, inverse,
    )
    new_a = out_a.transpose(1, 0, 2).reshape(16, 2, 4, N)
    new_b = out_b.transpose(1, 0, 2).reshape(16, 2, 4, N)
    zonal = out_z[0].reshape(12, 2, 16)[:, 0, :].T
    return (new_a, new_b, zonal)


def solution(mesh):
    return jax.shard_map(
        shards,
        mesh=mesh,
        in_specs=(
            P("row", None, "ma", None),
            P("row", None, "ma", None),
            P(),
            P("ma", None, None),
            P(),
            P(),
            P("row", None),
            P(),
            P("row", None, None),
        ),
        out_specs=(P("row", None, "ma", None), P("row", None, "ma", None), P("row", "ma")),
        check_vma=False,
    )
```

profile of v0, /device:TPU:1, one launch (start us, length us, event | category | flops | bytes accessed | tf_op | source)
XLA Modules:
  0.0 132.4 jit_solution(378779862657897322)
XLA Ops:
  0.6 0.7 reshape.26.qw
  1.3 0.7 reshape.27.colat
  2.0 0.7 reshape.25.theta_v
  2.7 0.0 copy-start
  2.7 1.9 %copy-done = bf16[24,256,256]{2,1,0:T(8,128)(2,1)S(1)} copy-done((bf16[24,256,256]{2,1,0:T(8,128)(2,1)S(1)}, bf16[24,256,256]{2,1,0:T(8,128)(2,1)}, u32[]{:S(2)}) %copy-start) | copy-done | bytes 3145752
  4.6 0.0 copy-start.1
  4.6 1.3 copy-done.1
  5.8 0.0 copy-start.2
  5.8 0.9 copy-done.2
  6.8 0.0 copy-start.3
  6.8 0.9 copy-done.3
  7.7 0.0 copy-start.4
  7.7 0.7 copy-done.4
  8.4 0.0 copy-start.5
  8.4 0.7 copy-done.5
  9.1 0.0 copy-start.6
  9.1 0.7 copy-done.6
  9.8 119.9 %shell_steps.1 = (f32[3,128,128]{2,1,0:T(8,128)S(1)}, f32[3,128,128]{2,1,0:T(8,128)S(1)}, f32[8,384]{1,0:T(8,128)S(1)}) custom-call(f32[16,2,4,384]{3,2,1,0:T(4,128)S(1)} %copy-done.2, f32[16,2,4,384]{3,2,1,0:T(4,128)S(1)} %copy-done.3, s32[128]{0:T(128)S(1)} %copy-done.6, s32[384]{0:T(512)S(1)} %copy-done.5, s32[1,128]{1,0:T(1,128)S(1)} %bitcast.8, ...), custom_call_target="tpu_custom_call" | custom-call | tf_op jit(solution)/shard_map/shell_steps/pallas_call | solution.py:275
  129.7 0.1 reshape_squeeze.3
  129.8 0.7 copy.16
  130.5 0.1 copy.14
  130.6 0.8 reshape.29
  131.5 0.1 copy.13
  131.6 0.8 reshape.28
  (2 shorter events, 0.0 us)
Async XLA Ops:
  2.7 1.9 %copy-start = (bf16[24,256,256]{2,1,0:T(8,128)(2,1)S(1)}, bf16[24,256,256]{2,1,0:T(8,128)(2,1)}, u32[]{:S(2)}) copy-start(bf16[24,256,256]{2,1,0:T(8,128)(2,1)} %inv_hbm.1) | copy-start | bytes 9437188
  4.6 1.3 copy-start.1
  5.8 0.9 copy-start.2
  6.8 0.9 copy-start.3
  7.7 0.7 copy-start.4
  8.4 0.7 copy-start.5
  9.1 0.7 copy-start.6
where the time goes:
time: 133 us; the launch traced here: 132 us
  Pallas kernels  120 us (90%)
  local copies, waits for them, and re-layouts  11.8 us (9%)
    pallas_call x1, Pallas kernels, shards(): pl.pallas_call(kernel, out_shape=(jax.ShapeDtypeStruct((3, 128, 128), F32...  120 us
    unnamed x15, local copies, waits for them, and re-layouts  7.76 us

commit v1 on v0

v1 whole, which is shorter than its diff:
```python
import math

import jax
import jax.numpy as jnp
from jax import lax
from jax.experimental import pallas as pl
from jax.experimental.pallas import tpu as pltpu
from jax.sharding import PartitionSpec as P

STEPS = 3
NPHI = 768
N = 384
NMA = 32
NROW = 16
F32 = jnp.float32
BF16 = jnp.bfloat16
MESH = pl.DeviceIdType.MESH


def iota(shape, dim):
    return lax.broadcasted_iota(jnp.int32, shape, dim)


def dot(a, b):
    return jnp.dot(a, b, preferred_element_type=F32)


def onehot(test):
    return jnp.where(test, 1.0, 0.0).astype(BF16)


def exact_dot(a, hot):
    hi = a.astype(BF16)
    rest = a - hi.astype(F32)
    mid = rest.astype(BF16)
    low = (rest - mid.astype(F32)).astype(BF16)
    return dot(hi, hot) + dot(mid, hot) + dot(low, hot)


def far_first(count):
    return sorted(range(count), key=lambda d: -min(d, count - d))


def farthest(first, second):
    pairs = [(a, b) for a in far_first(first) for b in far_first(second)]
    pairs.sort(key=lambda p: -min(p[0], first - p[0]) - min(p[1], second - p[1]))
    return pairs[:-1]


def kernel(
    fa_hbm, fb_hbm, ids_hbm, theta_hbm, leg_hbm, qw_hbm, colat_hbm, lor_hbm, inv_hbm,
    out_a, out_b, out_z,
    fa, fb, leg, lor, ids_s, theta_s, ids_v, theta_v, qw, colat,
    legp, wp, spec, xs, tt, bt, val, k1, k2, force, yf, zt, gs, g, ms, h, rs, c, us, s, inv, pick,
    send_sem, recv_sem, load_sem,
):
    row = lax.axis_index("row")
    ma = lax.axis_index("ma")
    ma_x, ma_z = ma // 8, lax.rem(ma, 8)
    row_y, row_core = row // 2, lax.rem(row, 2)
    on_x = [lax.rem(ma_x + d, 4) * 8 for d in range(4)]
    on_z = [lax.rem(ma_z + d, 8) for d in range(8)]
    on_y = [lax.rem(row_y + d, 8) * 2 for d in range(8)]
    on_core = [row_core, 1 - row_core]
    ma_others = [on_x[a] + on_z[b] for a, b in farthest(4, 8)]
    row_others = [on_y[a] + on_core[b] for a in far_first(8) for b in (1, 0) if (a, b) != (0, 0)]

    loads = [
        pltpu.make_async_copy(src, dst, load_sem.at[i])
        for i, (src, dst) in enumerate((
            (theta_hbm, theta_v), (leg_hbm, leg), (ids_hbm, ids_s), (fa_hbm, fa), (fb_hbm, fb), (theta_hbm, theta_s),
            (ids_hbm, ids_v), (colat_hbm, colat), (lor_hbm, lor), (qw_hbm, qw), (inv_hbm, inv),
        ))
    ]
    for load in loads:
        load.start()

    barrier = pltpu.get_barrier_semaphore()

    def greet_ma(i, _):
        pl.semaphore_signal(barrier, inc=1, device_id={"ma": lax.rem(ma + i, NMA)}, device_id_type=MESH)
        return 0

    def greet_row(i, _):
        pl.semaphore_signal(barrier, inc=1, device_id={"row": lax.rem(row + i, NROW)}, device_id_type=MESH)
        return 0

    lax.fori_loop(1, NMA, greet_ma, 0)
    lax.fori_loop(1, NROW, greet_row, 0)

    lane = iota((1, N), 1)
    lane128 = iota((1, 128), 1)
    degree = (lane & 15) * 24 + (lane >> 4)

    def live(m):
        return degree >= ids_s[ma * 4 + m]

    to_degree = onehot(iota((N, N), 0) == degree)
    shuffle = onehot(iota((N, N), 0) == (lane & 31) * 12 + (lane >> 5))
    loads[0].wait()
    nat = onehot(iota((N, N), 0) == theta_v[...].reshape(1, N))
    pick[...] = jnp.transpose(dot(nat, shuffle)).astype(BF16)
    loads[1].wait()
    for m in range(4):
        legp[m] = dot(pick[...], dot(leg[m], to_degree).astype(BF16)).astype(BF16)

    for load in loads[2:5]:
        load.wait()
    for m in range(4):
        for part in range(2):
            for f, field in ((0, fa), (1, fb)):
                piece = field[:, part, m, :]
                hi = piece.astype(BF16)
                lo = (piece - hi.astype(F32)).astype(BF16)
                moved = jnp.where(live(m), dot(hi, to_degree) + dot(lo, to_degree), 0.0)
                spec[m * 4 + part * 2 + f] = moved
                xs[m * 4 + part * 2 + f] = moved.astype(BF16)

    pl.semaphore_wait(barrier, NMA + NROW - 2)

    def cols(q):
        return slice(q * 128, q * 128 + 128)

    def send(src, dst, k, q, axis, me, others):
        for to in others:
            pltpu.make_async_remote_copy(
                src_ref=src.at[to, :, cols(q)],
                dst_ref=dst.at[me, :, cols(q)],
                send_sem=send_sem.at[k, q],
                recv_sem=recv_sem.at[k, q],
                device_id={axis: to},
                device_id_type=MESH,
            ).start()
        dst[me, :, cols(q)] = src[me, :, cols(q)]

    def send_ma(src, dst, k, q):
        send(src, dst, k, q, "ma", ma, ma_others)

    def send_row(src, dst, k, q):
        send(src, dst, k, q, "row", row, row_others)

    def arrive(dst, count, k, q):
        rest = dst.at[pl.ds(0, count - 1), :, cols(q)]
        pltpu.make_async_copy(rest, rest, recv_sem.at[k, q]).wait()

    def sent(src, count, k):
        for q in range(3):
            rest = src.at[pl.ds(0, count - 1), :, cols(q)]
            pltpu.make_async_copy(rest, rest, send_sem.at[k, q]).wait()

    def swap16(parts):
        parts = list(parts)
        for k in (1, 2, 4, 8):
            low = (lane128 & k) == 0
            for i in range(16):
                if i & k == 0:
                    a, b = parts[i], parts[i + k]
                    parts[i] = jnp.where(low, a, pltpu.roll(b, k, 1))
                    parts[i + k] = jnp.where(low, pltpu.roll(a, 128 - k, 1), b)
        return parts

    def prepare_longitude():
        for load in loads[5:9]:
            load.wait()
        n = iota((1, 256), 1)
        expand = onehot(iota((128, 256), 0) == (n >> 3) * 4 + (n & 3))
        ids = jnp.broadcast_to(ids_v[...].reshape(1, 128), (8, 128))
        top = ids >> 4
        mode = 16.0 * dot(top.astype(F32).astype(BF16), expand) + dot((ids & 15).astype(F32).astype(BF16), expand)
        mode = mode[0:1]

        def angles(count, period):
            k = mode * iota((count, 256), 0).astype(F32)
            k = k - period * jnp.floor((k + 0.5) * (1.0 / period))
            k = jnp.where(k > period / 2, k - period, k)
            return k * (2.0 * math.pi / period)

        coarse = angles(24, 24)
        fine = angles(32, NPHI)
        cos_c, sin_c = jnp.cos(coarse), jnp.sin(coarse)
        cos_f, sin_f = jnp.cos(fine), jnp.sin(fine)
        is_cos = (n & 4) == 0
        lead_c = jnp.where(is_cos, cos_c, -sin_c)
        lead_s = jnp.where(is_cos, sin_c, cos_c)
        for a in range(24):
            value = lead_c[a:a + 1] * cos_f - lead_s[a:a + 1] * sin_f
            val[a * 32:a * 32 + 32, :] = value
            tt[a * 32:a * 32 + 32, :] = (value * (1.0 / math.sqrt(128))).astype(BF16)
        for a in range(3):
            bt[:, a * 256:a * 256 + 256] = (
                jnp.transpose(val[a * 256:a * 256 + 256, :]) * math.sqrt(2.0 / NPHI)
            ).astype(BF16)

        own = jnp.zeros((1, N), jnp.int32)
        for t in range(12):
            own = jnp.where((lane >> 5) == t, theta_s[ma * 12 + t], own)
        hot = onehot(iota((N, N), 0) == own)
        is_a = (lane & 16) == 0
        cosines = exact_dot(jnp.broadcast_to(colat[...].reshape(1, N), (8, N)), hot)[0:1]
        k1[...] = jnp.where(is_a, 2.0 * cosines, -2.0 * cosines)
        energy = exact_dot(lor[...], hot)
        energy = jnp.sum(jnp.where(iota((16, N), 0) == (lane & 15), energy, 0.0), axis=0, keepdims=True)
        k2[...] = jnp.where(is_a, energy, 1.0)

    def prepare_weighted():
        loads[9].wait()
        column = jnp.transpose(jnp.broadcast_to(qw[...].reshape(1, N), (128, N)))[:, 0:1]
        for m in range(4):
            w = (column * leg[m].astype(F32)).astype(BF16)
            w = dot(pick[...], dot(w, to_degree).astype(BF16))
            wp[m] = jnp.where(live(m), w, 0.0).astype(BF16)

    def step(n, _):
        for q in range(3):
            for m in range(4):
                x0 = xs[m * 4:m * 4 + 2].reshape(32, N)
                x1 = xs[m * 4 + 2:m * 4 + 4].reshape(32, N)
                x = jnp.concatenate([x0] * 4 + [x1] * 4, axis=0)
                y = lax.dot_general(
                    legp[m, cols(q), :], x, (((1,), (1,)), ((), ())), preferred_element_type=F32
                )
                for part in range(2):
                    piece = y[0:32, cols(part)]
                    for j in range(1, 4):
                        piece = jnp.where((lane128 >> 5) == j, y[j * 32:j * 32 + 32, cols(part)], piece)
                    yf[q, pl.ds(part * 4 + m, 32, stride=8), :] = piece
            gs[:, :, cols(q)] = yf[q].reshape(NMA, 8, 128).astype(BF16)
            send_ma(gs, g, 0, q)
        pl.when(n == 0)(prepare_longitude)

        for q in range(3):
            arrive(g, NMA, 0, q)
            grid = g[:, :, cols(q)].astype(F32).reshape(256, 128)
            other = jnp.where((lane128 & 16) == 0, pltpu.roll(grid, 112, 1), pltpu.roll(grid, 16, 1))
            both = jnp.concatenate([grid, other], axis=1).astype(BF16)
            total = jnp.zeros((1, 128), F32)
            for a in range(3):
                phys = dot(tt[a * 256:a * 256 + 256, :], both)
                value = phys[:, 128:] * (k1[:, cols(q)] + k2[:, cols(q)] * phys[:, :128])
                force[a * 256:a * 256 + 256, cols(q)] = value.astype(BF16)
                total = total + jnp.sum(value, axis=0, keepdims=True)
            out_z[:, cols(q)] = jnp.broadcast_to(total * (1.0 / NPHI), (8, 128))
            ms[:, :, cols(q)] = dot(bt[...], force[:, cols(q)]).reshape(NMA, 8, 128).astype(BF16)
            send_ma(ms, h, 1, q)
        pl.when(n == 0)(prepare_weighted)

        for q in range(3):
            arrive(h, NMA, 1, q)
            yf[q] = h[:, :, cols(q)].astype(F32).reshape(256, 128)
            for m in range(4):
                pieces = []
                for j in range(4):
                    p0 = yf[q, pl.ds(m, 32, stride=8), :]
                    p1 = yf[q, pl.ds(4 + m, 32, stride=8), :]
                    if j != 0:
                        p0 = pltpu.roll(p0, 128 - 32 * j, 1)
                    if j != 1:
                        p1 = pltpu.roll(p1, (160 - 32 * j) % 128, 1)
                    pieces.append(jnp.where(lane128 < 32, p0, p1))
                zt[m, :, cols(q)] = jnp.transpose(jnp.concatenate(pieces, axis=0))[0:64].astype(BF16)
        sent(gs, NMA, 0)
        for q in range(3):
            parts = []
            for m in range(4):
                term = (0.25 * dot(zt[m], wp[m, :, cols(q)])).astype(BF16).astype(F32)
                total = spec[m * 4:m * 4 + 4, :, cols(q)].reshape(64, 128) + term
                total = total.astype(BF16).astype(F32)
                parts += [total[i * 16:i * 16 + 16] for i in range(4)]
            for i, part in enumerate(swap16(parts)):
                rs[i, :, cols(q)] = part.astype(BF16)
            send_row(rs, c, 2, q)
        sent(ms, NMA, 1)
        pl.when(n == 0)(loads[10].wait)

        for q in range(3):
            arrive(c, NROW, 2, q)
            right = c[:, :, cols(q)].reshape(256, 128)
            solved = dot(inv[q * 8], right)
            for i in range(1, 8):
                solved = jnp.where((lane128 >> 4) == i, dot(inv[q * 8 + i], right), solved)
            us[:, :, cols(q)] = solved.astype(BF16).reshape(NROW, 16, 128)
            send_row(us, s, 3, q)
        sent(rs, NROW, 2)
        for q in range(3):
            arrive(s, NROW, 3, q)
            for i, part in enumerate(swap16([s[i, :, cols(q)].astype(F32) for i in range(16)])):
                spec[i, :, cols(q)] = part
                xs[i, :, cols(q)] = part.astype(BF16)
        sent(us, NROW, 3)
        return 0

    lax.fori_loop(0, STEPS, step, 0)

    from_degree = onehot((iota((N, N), 0) & 15) * 24 + (iota((N, N), 0) >> 4) == iota((N, N), 1))
    result = dot(xs[...].reshape(256, N), from_degree)
    for m in range(4):
        for part in range(2):
            for f, out in ((0, out_a), (1, out_b)):
                i = m * 4 + part * 2 + f
                for q in range(3):
                    out[q, pl.ds(part * 4 + m, 16, stride=8), :] = result[i * 16:i * 16 + 16, cols(q)]


def shards(
    field_a, field_b, mode_ids, legendre, quad_weights, colat_cos, lorentz, theta_order, inverse
):
    vmem = pl.BlockSpec(memory_space=pltpu.VMEM)
    hbm = pl.BlockSpec(memory_space=pltpu.HBM)
    out_a, out_b, out_z = pl.pallas_call(
        kernel,
        out_shape=(
            jax.ShapeDtypeStruct((3, 128, 128), F32),
            jax.ShapeDtypeStruct((3, 128, 128), F32),
            jax.ShapeDtypeStruct((8, N), F32),
        ),
        in_specs=[hbm] * 9,
        out_specs=(vmem, vmem, vmem),
        scratch_shapes=[
            pltpu.VMEM((16, 2, 4, N), F32),
            pltpu.VMEM((16, 2, 4, N), F32),
            pltpu.VMEM((4, N, N), BF16),
            pltpu.VMEM((16, N), F32),
            pltpu.SMEM((128,), jnp.int32),
            pltpu.SMEM((N,), jnp.int32),
            pltpu.VMEM((128,), jnp.int32),
            pltpu.VMEM((N,), jnp.int32),
            pltpu.VMEM((N,), F32),
            pltpu.VMEM((N,), F32),
            pltpu.VMEM((4, N, N), BF16),
            pltpu.VMEM((4, N, N), BF16),
            pltpu.VMEM((16, 16, N), F32),
            pltpu.VMEM((16, 16, N), BF16),
            pltpu.VMEM((NPHI, 256), BF16),
            pltpu.VMEM((256, NPHI), BF16),
            pltpu.VMEM((NPHI, 256), F32),
            pltpu.VMEM((1, N), F32),
            pltpu.VMEM((1, N), F32),
            pltpu.VMEM((NPHI, N), BF16),
            pltpu.VMEM((3, 256, 128), F32),
            pltpu.VMEM((4, 64, N), BF16),
            pltpu.VMEM((NMA, 8, N), BF16),
            pltpu.VMEM((NMA, 8, N), BF16),
            pltpu.VMEM((NMA, 8, N), BF16),
            pltpu.VMEM((NMA, 8, N), BF16),
            pltpu.VMEM((NROW, 16, N), BF16),
            pltpu.VMEM((NROW, 16, N), BF16),
            pltpu.VMEM((NROW, 16, N), BF16),
            pltpu.VMEM((NROW, 16, N), BF16),
            pltpu.VMEM((24, 256, 256), BF16),
            pltpu.VMEM((N, N), BF16),
            pltpu.SemaphoreType.DMA((4, 3)),
            pltpu.SemaphoreType.DMA((4, 3)),
            pltpu.SemaphoreType.DMA((11,)),
        ],
        compiler_params=pltpu.CompilerParams(
            collective_id=0, has_side_effects=True, vmem_limit_bytes=64 * 1024 * 1024
        ),
        name="shell_steps",
    )(
        field_a, field_b, mode_ids, theta_order, legendre, quad_weights, colat_cos, lorentz, inverse,
    )
    new_a = out_a.transpose(1, 0, 2).reshape(16, 2, 4, N)
    new_b = out_b.transpose(1, 0, 2).reshape(16, 2, 4, N)
    zonal = out_z[0].reshape(12, 2, 16)[:, 0, :].T
    return (new_a, new_b, zonal)


def solution(mesh):
    return jax.shard_map(
        shards,
        mesh=mesh,
        in_specs=(
            P("row", None, "ma", None),
            P("row", None, "ma", None),
            P(),
            P("ma", None, None),
            P(),
            P(),
            P("row", None),
            P(),
            P("row", None, None),
        ),
        out_specs=(P("row", None, "ma", None), P("row", None, "ma", None), P("row", "ma")),
        check_vma=False,
    )
```

time: 133 us -> 110 us (0.83)
  Pallas kernels: 120 us -> 104 us
  local copies, waits for them, and re-layouts: 11.8 us -> 5.26 us
    pallas_call x1, Pallas kernels: 120 us -> 104 us  [shards(): pl.pallas_call(kernel, out_shape=(jax.ShapeDtypeStruct((3, 128, 128), F32...]
    unnamed x15 -> x1, local copies, waits for them, and re-layouts: 7.76 us -> 0.68 us
    reshape x3 -> x0, local copies, waits for them, and re-layouts: 2.05 us -> none  [the longest x1 0.68 us: shards(): quad_weights.reshape(1, N)]
where the time goes in v1:
time: 110 us
  Pallas kernels  104 us (95%)
  local copies, waits for them, and re-layouts  5.26 us (5%)
    pallas_call x1, Pallas kernels, shards(): pl.pallas_call(kernel, out_shape=(jax.ShapeDtypeStruct((3, 128, 128), F32...  104 us

profile of v1, /device:TPU:1, one launch (start us, length us, event | category | flops | bytes accessed | tf_op | source)
XLA Modules:
  0.0 109.7 jit_solution(3083985151130252543)
XLA Ops:
  0.6 103.8 %shell_steps.1 = (f32[3,128,128]{2,1,0:T(8,128)}, f32[3,128,128]{2,1,0:T(8,128)}, f32[8,384]{1,0:T(8,128)}) custom-call(f32[16,2,4,384]{3,2,1,0:T(4,128)} %fa_hbm.1, f32[16,2,4,384]{3,2,1,0:T(4,128)} %fb_hbm.1, s32[128]{0:T(128)} %ids_hbm.1, s32[384]{0:T(512)} %theta_hbm.1, bf16[4,384,384]{2,1,0:T(8,128)(2,1)} %leg_hbm.1, f32[384]{0:T(512)} %qw_hbm.1, ...), custom_call_target="tpu_custom_call" | custom-call | tf_op jit(solution)/shard_map/shell_steps/pallas_call | solution.py:309
  104.4 0.7 slice_reduce_fusion
  105.2 0.1 reshape_squeeze.3
  105.3 0.7 copy.16
  105.9 1.1 copy.14
  107.0 0.8 reshape.13
  107.8 1.1 copy.13
  108.9 0.8 reshape.12
  (1 shorter events, 0.0 us)

commit v2 on v1

v2 whole, which is shorter than its diff:
```python
import math

import jax
import jax.numpy as jnp
from jax import lax
from jax.experimental import pallas as pl
from jax.experimental.pallas import tpu as pltpu
from jax.sharding import PartitionSpec as P

STEPS = 3
NPHI = 768
N = 384
NMA = 32
NROW = 16
MA_PIECES = ((0, 1), (1, 3))
ROW_PIECES = ((0, 1), (1, 3))
F32 = jnp.float32
BF16 = jnp.bfloat16
MESH = pl.DeviceIdType.MESH


def iota(shape, dim):
    return lax.broadcasted_iota(jnp.int32, shape, dim)


def dot(a, b):
    return jnp.dot(a, b, preferred_element_type=F32)


def onehot(test):
    return jnp.where(test, 1.0, 0.0).astype(BF16)


def exact_dot(a, hot):
    hi = a.astype(BF16)
    rest = a - hi.astype(F32)
    mid = rest.astype(BF16)
    low = (rest - mid.astype(F32)).astype(BF16)
    return dot(hi, hot) + dot(mid, hot) + dot(low, hot)


def far_first(count):
    return sorted(range(count), key=lambda d: -min(d, count - d))


def farthest(first, second):
    pairs = [(a, b) for a in far_first(first) for b in far_first(second)]
    pairs.sort(key=lambda p: -min(p[0], first - p[0]) - min(p[1], second - p[1]))
    return pairs[:-1]


def kernel(
    fa_hbm, fb_hbm, ids_hbm, theta_hbm, leg_hbm, qw_hbm, colat_hbm, lor_hbm, inv_hbm,
    xs, out_z,
    fa, fb, leg, lor, ids_s, theta_s, ids_v, theta_v, qw, colat,
    legp, wp, spec, tt, bt, val, k1, k2, force, yf, zt, back, gs, g, ms, h, rs, c, us, s, inv, pick,
    send_sem, recv_sem, load_sem,
):
    row = lax.axis_index("row")
    ma = lax.axis_index("ma")
    ma_x, ma_z = ma // 8, lax.rem(ma, 8)
    row_y, row_core = row // 2, lax.rem(row, 2)
    on_x = [lax.rem(ma_x + d, 4) * 8 for d in range(4)]
    on_z = [lax.rem(ma_z + d, 8) for d in range(8)]
    on_y = [lax.rem(row_y + d, 8) * 2 for d in range(8)]
    on_core = [row_core, 1 - row_core]
    ma_others = [on_x[a] + on_z[b] for a, b in farthest(4, 8)]
    row_others = [on_y[a] + on_core[b] for a in far_first(8) for b in (1, 0) if (a, b) != (0, 0)]

    barrier = pltpu.get_barrier_semaphore()
    for to in ma_others:
        pl.semaphore_signal(barrier, inc=1, device_id={"ma": to}, device_id_type=MESH)
    for to in row_others:
        pl.semaphore_signal(barrier, inc=1, device_id={"row": to}, device_id_type=MESH)

    loads = [
        pltpu.make_async_copy(src, dst, load_sem.at[i])
        for i, (src, dst) in enumerate((
            (theta_hbm, theta_v), (leg_hbm, leg), (ids_hbm, ids_s), (fa_hbm, fa), (fb_hbm, fb), (theta_hbm, theta_s),
            (ids_hbm, ids_v), (colat_hbm, colat), (lor_hbm, lor), (qw_hbm, qw), (inv_hbm, inv),
        ))
    ]
    for load in loads:
        load.start()

    lane = iota((1, N), 1)
    lane128 = iota((1, 128), 1)
    degree = (lane & 15) * 24 + (lane >> 4)

    shuffle = onehot(iota((N, N), 0) == (lane & 31) * 12 + (lane >> 5))
    loads[0].wait()
    nat = onehot(iota((N, N), 0) == theta_v[...].reshape(1, N))
    pick[...] = jnp.transpose(dot(nat, shuffle)).astype(BF16)
    for load in loads[1:5]:
        load.wait()
    for m in range(4):
        legp[m] = dot(pick[...], leg[m]).astype(BF16)
        alive = lane >= ids_s[ma * 4 + m]
        for part in range(2):
            for f, field in ((0, fa), (1, fb)):
                xs[m * 4 + part * 2 + f] = jnp.where(alive, field[:, part, m, :], 0.0).astype(BF16)

    pl.semaphore_wait(barrier, NMA + NROW - 2)

    def cols(q):
        return slice(q * 128, q * 128 + 128)

    def columns(piece):
        return slice(piece[0] * 128, piece[1] * 128)

    def send(src, dst, k, i, axis, me, others, pieces):
        block = columns(pieces[i])
        for to in others:
            pltpu.make_async_remote_copy(
                src_ref=src.at[to, :, block],
                dst_ref=dst.at[me, :, block],
                send_sem=send_sem.at[k, i],
                recv_sem=recv_sem.at[k, i],
                device_id={axis: to},
                device_id_type=MESH,
            ).start()
        dst[me, :, block] = src[me, :, block]

    def send_ma(src, dst, k, i):
        send(src, dst, k, i, "ma", ma, ma_others, MA_PIECES)

    def send_row(src, dst, k, i):
        send(src, dst, k, i, "row", row, row_others, ROW_PIECES)

    def finish(ref, sem, piece):
        rest = ref.at[pl.ds(0, ref.shape[0] - 1), :, columns(piece)]
        pltpu.make_async_copy(rest, rest, sem).wait()

    def arrive(dst, k, i):
        finish(dst, recv_sem.at[k, i], (MA_PIECES if k < 2 else ROW_PIECES)[i])

    def sent(src, k):
        for i, piece in enumerate(MA_PIECES if k < 2 else ROW_PIECES):
            finish(src, send_sem.at[k, i], piece)

    def swap16(parts):
        parts = list(parts)
        for k in (1, 2, 4, 8):
            low = (lane128 & k) == 0
            for i in range(16):
                if i & k == 0:
                    a, b = parts[i], parts[i + k]
                    parts[i] = jnp.where(low, a, pltpu.roll(b, k, 1))
                    parts[i + k] = jnp.where(low, pltpu.roll(a, 128 - k, 1), b)
        return parts

    def to_degree():
        return onehot(iota((N, N), 0) == degree)

    def prepare_spectral():
        hot = to_degree()
        for m in range(4):
            legp[m] = dot(legp[m], hot).astype(BF16)
            alive = lane >= ids_s[ma * 4 + m]
            for part in range(2):
                for f, field in ((0, fa), (1, fb)):
                    piece = jnp.where(alive, field[:, part, m, :], 0.0)
                    hi = piece.astype(BF16)
                    lo = (piece - hi.astype(F32)).astype(BF16)
                    spec[m * 4 + part * 2 + f] = dot(hi, hot) + dot(lo, hot)

    def prepare_longitude():
        for load in loads[5:9]:
            load.wait()
        n = iota((1, 256), 1)
        expand = onehot(iota((128, 256), 0) == (n >> 3) * 4 + (n & 3))
        ids = jnp.broadcast_to(ids_v[...].reshape(1, 128), (8, 128))
        top = ids >> 4
        mode = 16.0 * dot(top.astype(F32).astype(BF16), expand) + dot((ids & 15).astype(F32).astype(BF16), expand)
        mode = mode[0:1]

        def angles(count, period):
            k = mode * iota((count, 256), 0).astype(F32)
            k = k - period * jnp.floor((k + 0.5) * (1.0 / period))
            k = jnp.where(k > period / 2, k - period, k)
            return k * (2.0 * math.pi / period)

        coarse = angles(24, 24)
        fine = angles(32, NPHI)
        cos_c, sin_c = jnp.cos(coarse), jnp.sin(coarse)
        cos_f, sin_f = jnp.cos(fine), jnp.sin(fine)
        is_cos = (n & 4) == 0
        lead_c = jnp.where(is_cos, cos_c, -sin_c)
        lead_s = jnp.where(is_cos, sin_c, cos_c)
        for a in range(24):
            value = lead_c[a:a + 1] * cos_f - lead_s[a:a + 1] * sin_f
            val[a * 32:a * 32 + 32, :] = value
            tt[a * 32:a * 32 + 32, :] = (value * (1.0 / math.sqrt(128))).astype(BF16)
        for a in range(3):
            bt[:, a * 256:a * 256 + 256] = (
                jnp.transpose(val[a * 256:a * 256 + 256, :]) * math.sqrt(2.0 / NPHI)
            ).astype(BF16)

        own = jnp.zeros((1, N), jnp.int32)
        for t in range(12):
            own = jnp.where((lane >> 5) == t, theta_s[ma * 12 + t], own)
        hot = onehot(iota((N, N), 0) == own)
        is_a = (lane & 16) == 0
        cosines = exact_dot(jnp.broadcast_to(colat[...].reshape(1, N), (8, N)), hot)[0:1]
        k1[...] = jnp.where(is_a, 2.0 * cosines, -2.0 * cosines)
        energy = exact_dot(lor[...], hot)
        energy = jnp.sum(jnp.where(iota((16, N), 0) == (lane & 15), energy, 0.0), axis=0, keepdims=True)
        k2[...] = jnp.where(is_a, energy, 1.0)

    def prepare_weighted():
        loads[9].wait()
        hot = to_degree()
        column = jnp.transpose(jnp.broadcast_to(qw[...].reshape(1, N), (128, N)))[:, 0:1]
        for m in range(4):
            w = (column * leg[m].astype(F32)).astype(BF16)
            w = dot(pick[...], dot(w, hot).astype(BF16))
            w = jnp.where(degree >= ids_s[ma * 4 + m], w, 0.0).astype(BF16)
            for t in range(12):
                wp[t * 128 + m * 32:t * 128 + m * 32 + 32, :] = w[t * 32:t * 32 + 32]

    zt[...] = jnp.zeros_like(zt)

    def step(n, _):
        for i, piece in enumerate(MA_PIECES):
            low, high = piece
            for m in range(4):
                x0 = xs[m * 4:m * 4 + 2].reshape(32, N)
                x1 = xs[m * 4 + 2:m * 4 + 4].reshape(32, N)
                x = jnp.concatenate([x0] * 4 + [x1] * 4, axis=0)
                y = lax.dot_general(
                    legp[m, columns(piece), :], x, (((1,), (1,)), ((), ())), preferred_element_type=F32
                )
                for part in range(2):
                    for q in range(low, high):
                        first = (q - low) * 128
                        block = y[first:first + 32, cols(part)]
                        for j in range(1, 4):
                            other = y[first + j * 32:first + j * 32 + 32, cols(part)]
                            block = jnp.where((lane128 >> 5) == j, other, block)
                        yf[q, pl.ds(part * 4 + m, 32, stride=8), :] = block
            for q in range(low, high):
                gs[:, :, cols(q)] = yf[q].reshape(NMA, 8, 128).astype(BF16)
            send_ma(gs, g, 0, i)
        pl.when(n == 0)(prepare_longitude)
        pl.when(n == 0)(prepare_spectral)

        for i, piece in enumerate(MA_PIECES):
            arrive(g, 0, i)
            width = (piece[1] - piece[0]) * 128
            block = columns(piece)
            grids = [g[:, :, cols(q)].astype(F32).reshape(256, 128) for q in range(*piece)]
            others = [
                jnp.where((lane128 & 16) == 0, pltpu.roll(v, 112, 1), pltpu.roll(v, 16, 1)) for v in grids
            ]
            both = jnp.concatenate(grids + others, axis=1).astype(BF16)
            total = jnp.zeros((1, width), F32)
            for a in range(3):
                phys = dot(tt[a * 256:a * 256 + 256, :], both)
                value = phys[:, width:] * (k1[:, block] + k2[:, block] * phys[:, :width])
                force[a * 256:a * 256 + 256, block] = value.astype(BF16)
                total = total + jnp.sum(value, axis=0, keepdims=True)
            out_z[:, block] = jnp.broadcast_to(total * (1.0 / NPHI), (8, width))
            ms[:, :, block] = dot(bt[...], force[:, block]).reshape(NMA, 8, width).astype(BF16)
            send_ma(ms, h, 1, i)
        pl.when(n == 0)(prepare_weighted)

        for i, piece in enumerate(MA_PIECES):
            arrive(h, 1, i)
            for q in range(*piece):
                yf[q] = h[:, :, cols(q)].astype(F32).reshape(256, 128)
                for part in range(2):
                    stack = [yf[q, pl.ds(part * 4 + m, 32, stride=8), :] for m in range(4)]
                    turned = jnp.transpose(jnp.concatenate(stack, axis=0)).astype(BF16)
                    for m in range(4):
                        for j in range(4):
                            first = (q * 4 + j) * 128 + m * 32
                            zt[m * 64 + part * 32:m * 64 + part * 32 + 32, first:first + 32] = (
                                turned[j * 32:j * 32 + 32, m * 32:m * 32 + 32]
                            )
            if i == 0:
                early = slice(0, piece[1] * 512)
                late = slice(piece[1] * 512, 1536)
                back[...] = dot(zt[:, early], wp[early, :])
        sent(gs, 0)
        for i, piece in enumerate(ROW_PIECES):
            block = columns(piece)
            width = (piece[1] - piece[0]) * 128
            term = (0.25 * (back[:, block] + dot(zt[:, late], wp[late, block]))).astype(BF16).astype(F32)
            total = (spec[:, :, block].reshape(256, width) + term).astype(BF16).astype(F32)
            for q in range(*piece):
                parts = [total[j * 16:j * 16 + 16, cols(q - piece[0])] for j in range(16)]
                for j, part in enumerate(swap16(parts)):
                    rs[j, :, cols(q)] = part.astype(BF16)
            send_row(rs, c, 2, i)
        sent(ms, 1)
        pl.when(n == 0)(loads[10].wait)

        for i, piece in enumerate(ROW_PIECES):
            arrive(c, 2, i)
            for q in range(*piece):
                right = c[:, :, cols(q)].reshape(256, 128)
                solved = dot(inv[q * 8], right)
                for j in range(1, 8):
                    solved = jnp.where((lane128 >> 4) == j, dot(inv[q * 8 + j], right), solved)
                us[:, :, cols(q)] = solved.astype(BF16).reshape(NROW, 16, 128)
            send_row(us, s, 3, i)
        sent(rs, 2)
        for i, piece in enumerate(ROW_PIECES):
            arrive(s, 3, i)
            for q in range(*piece):
                for j, part in enumerate(swap16([s[j, :, cols(q)].astype(F32) for j in range(16)])):
                    spec[j, :, cols(q)] = part
                    xs[j, :, cols(q)] = part.astype(BF16)
        sent(us, 3)
        return 0

    lax.fori_loop(0, STEPS, step, 0)


def unload_kernel(xs, z, out_a, out_b, out_z):
    from_degree = onehot((iota((N, N), 0) & 15) * 24 + (iota((N, N), 0) >> 4) == iota((N, N), 1))
    result = dot(xs[...].reshape(256, N), from_degree)
    for m in range(4):
        for part in range(2):
            for f, out in ((0, out_a), (1, out_b)):
                i = m * 4 + part * 2 + f
                out[:, part, m, :] = result[i * 16:i * 16 + 16]
    lane = iota((16, N), 1)
    spread = jnp.where((lane & 31) == iota((16, N), 0), jnp.broadcast_to(z[0:1, :], (16, N)), 0.0)
    out_z[...] = exact_dot(spread, onehot((iota((N, 12), 0) >> 5) == iota((N, 12), 1)))


def shards(
    field_a, field_b, mode_ids, legendre, quad_weights, colat_cos, lorentz, theta_order, inverse
):
    vmem = pl.BlockSpec(memory_space=pltpu.VMEM)
    hbm = pl.BlockSpec(memory_space=pltpu.HBM)
    xs, z = pl.pallas_call(
        kernel,
        out_shape=(
            jax.ShapeDtypeStruct((16, 16, N), BF16),
            jax.ShapeDtypeStruct((8, N), F32),
        ),
        in_specs=[hbm] * 9,
        out_specs=(vmem, vmem),
        scratch_shapes=[
            pltpu.VMEM((16, 2, 4, N), F32),
            pltpu.VMEM((16, 2, 4, N), F32),
            pltpu.VMEM((4, N, N), BF16),
            pltpu.VMEM((16, N), F32),
            pltpu.SMEM((128,), jnp.int32),
            pltpu.SMEM((N,), jnp.int32),
            pltpu.VMEM((128,), jnp.int32),
            pltpu.VMEM((N,), jnp.int32),
            pltpu.VMEM((N,), F32),
            pltpu.VMEM((N,), F32),
            pltpu.VMEM((4, N, N), BF16),
            pltpu.VMEM((1536, N), BF16),
            pltpu.VMEM((16, 16, N), F32),
            pltpu.VMEM((NPHI, 256), BF16),
            pltpu.VMEM((256, NPHI), BF16),
            pltpu.VMEM((NPHI, 256), F32),
            pltpu.VMEM((1, N), F32),
            pltpu.VMEM((1, N), F32),
            pltpu.VMEM((NPHI, N), BF16),
            pltpu.VMEM((3, 256, 128), F32),
            pltpu.VMEM((256, 1536), BF16),
            pltpu.VMEM((256, N), F32),
            pltpu.VMEM((NMA, 8, N), BF16),
            pltpu.VMEM((NMA, 8, N), BF16),
            pltpu.VMEM((NMA, 8, N), BF16),
            pltpu.VMEM((NMA, 8, N), BF16),
            pltpu.VMEM((NROW, 16, N), BF16),
            pltpu.VMEM((NROW, 16, N), BF16),
            pltpu.VMEM((NROW, 16, N), BF16),
            pltpu.VMEM((NROW, 16, N), BF16),
            pltpu.VMEM((24, 256, 256), BF16),
            pltpu.VMEM((N, N), BF16),
            pltpu.SemaphoreType.DMA((4, 3)),
            pltpu.SemaphoreType.DMA((4, 3)),
            pltpu.SemaphoreType.DMA((11,)),
        ],
        compiler_params=pltpu.CompilerParams(
            collective_id=0, has_side_effects=True, vmem_limit_bytes=64 * 1024 * 1024
        ),
        name="shell_steps",
    )(
        field_a, field_b, mode_ids, theta_order, legendre, quad_weights, colat_cos, lorentz, inverse,
    )
    return pl.pallas_call(
        unload_kernel,
        out_shape=(
            jax.ShapeDtypeStruct((16, 2, 4, N), F32),
            jax.ShapeDtypeStruct((16, 2, 4, N), F32),
            jax.ShapeDtypeStruct((16, 12), F32),
        ),
        in_specs=[vmem, vmem],
        out_specs=(vmem, vmem, vmem),
        compiler_params=pltpu.CompilerParams(vmem_limit_bytes=64 * 1024 * 1024),
        name="unload",
    )(xs, z)


def solution(mesh):
    return jax.shard_map(
        shards,
        mesh=mesh,
        in_specs=(
            P("row", None, "ma", None),
            P("row", None, "ma", None),
            P(),
            P("ma", None, None),
            P(),
            P(),
            P("row", None),
            P(),
            P("row", None, None),
        ),
        out_specs=(P("row", None, "ma", None), P("row", None, "ma", None), P("row", "ma")),
        check_vma=False,
    )
```

time: 110 us -> 105 us (0.955)
  local copies, waits for them, and re-layouts: 5.26 us -> 0 us
    transpose x2 -> x0, local copies, waits for them, and re-layouts: 2.13 us -> none  [the longest x1 1.06 us: shards(): new_a = out_a.transpose(1, 0, 2).reshape(16, 2, 4, N)]
    reshape x2 -> x0, local copies, waits for them, and re-layouts: 1.63 us -> none  [the longest x1 0.82 us: shards(): new_b = out_b.transpose(1, 0, 2).reshape(16, 2, 4, N)]
    pallas_call x1 -> x2, Pallas kernels: 104 us -> 104 us  [the longest x1 102 us: shards(): pl.pallas_call(kernel, out_shape=(jax.ShapeDtypeStruct((16, 16, N), BF16)...]
where the time goes in v2:
time: 105 us; the launch traced here: 104 us
  Pallas kernels  104 us (99%)
    pallas_call x1, Pallas kernels, shards(): pl.pallas_call(kernel, out_shape=(jax.ShapeDtypeStruct((16, 16, N), BF16)...  102 us

profile of v2, /device:TPU:1, one launch (start us, length us, event | category | flops | bytes accessed | tf_op | source)
XLA Modules:
  0.0 104.4 jit_solution(26153244792396466)
XLA Ops:
  0.6 101.7 %shell_steps.1 = (bf16[16,16,384]{2,1,0:T(8,128)(2,1)}, f32[8,384]{1,0:T(8,128)}) custom-call(f32[16,2,4,384]{3,2,1,0:T(4,128)} %fa_hbm.1, f32[16,2,4,384]{3,2,1,0:T(4,128)} %fb_hbm.1, s32[128]{0:T(128)} %ids_hbm.1, s32[384]{0:T(512)} %theta_hbm.1, bf16[4,384,384]{2,1,0:T(8,128)(2,1)} %leg_hbm.1, f32[384]{0:T(512)} %qw_hbm.1, f32[384]{0:T(512)} %colat_hbm.1, ...), custom_call_target="tpu_custom_call" | custom-call | tf_op jit(solution)/shard_map/shell_steps/pallas_call | solution.py:338
  102.4 2.0 %unload.1 = (f32[16,2,4,384]{3,2,1,0:T(4,128)}, f32[16,2,4,384]{3,2,1,0:T(4,128)}, f32[16,12]{1,0:T(8,128)}) custom-call(bf16[16,16,384]{2,1,0:T(8,128)(2,1)} %get-tuple-element.5.xs, f32[8,384]{1,0:T(8,128)} %get-tuple-element.6.z), custom_call_target="tpu_custom_call" | custom-call | tf_op jit(solution)/shard_map/unload/pallas_call | solution.py:390

commit v3 on v2

--- a/solution.py
+++ b/solution.py
@@ -12,8 +12,7 @@
 N = 384
 NMA = 32
 NROW = 16
-MA_PIECES = ((0, 1), (1, 3))
-ROW_PIECES = ((0, 1), (1, 3))
+PIECES = (((0, 1), (1, 3)), ((0, 1), (1, 3)), ((0, 1), (1, 3)), ((0, 1), (1, 3)))
 F32 = jnp.float32
 BF16 = jnp.bfloat16
 MESH = pl.DeviceIdType.MESH
@@ -25,6 +24,11 @@
 
 def dot(a, b):
     return jnp.dot(a, b, preferred_element_type=F32)
+
+
+def degree_of(column):
+    holder = -column & 15
+    return holder * 24 + (column >> 7) * 8 + ((((column & 127) + holder) >> 4) & 7)
 
 
 def onehot(test):
@@ -47,6 +51,11 @@
     pairs = [(a, b) for a in far_first(first) for b in far_first(second)]
     pairs.sort(key=lambda p: -min(p[0], first - p[0]) - min(p[1], second - p[1]))
     return pairs[:-1]
+
+
+def units(arriving, leaving):
+    cuts = sorted({low for low, _ in arriving + leaving}) + [3]
+    return list(zip(cuts, cuts[1:]))
 
 
 def kernel(
@@ -85,7 +94,7 @@
 
     lane = iota((1, N), 1)
     lane128 = iota((1, 128), 1)
-    degree = (lane & 15) * 24 + (lane >> 4)
+    degree = degree_of(lane)
 
     shuffle = onehot(iota((N, N), 0) == (lane & 31) * 12 + (lane >> 5))
     loads[0].wait()
@@ -108,46 +117,45 @@
     def columns(piece):
         return slice(piece[0] * 128, piece[1] * 128)
 
-    def send(src, dst, k, i, axis, me, others, pieces):
-        block = columns(pieces[i])
-        for to in others:
-            pltpu.make_async_remote_copy(
-                src_ref=src.at[to, :, block],
-                dst_ref=dst.at[me, :, block],
-                send_sem=send_sem.at[k, i],
-                recv_sem=recv_sem.at[k, i],
-                device_id={axis: to},
-                device_id_type=MESH,
-            ).start()
-        dst[me, :, block] = src[me, :, block]
-
-    def send_ma(src, dst, k, i):
-        send(src, dst, k, i, "ma", ma, ma_others, MA_PIECES)
-
-    def send_row(src, dst, k, i):
-        send(src, dst, k, i, "row", row, row_others, ROW_PIECES)
+    def send(src, dst, k, done):
+        axis, me, others = ("ma", ma, ma_others) if k < 2 else ("row", row, row_others)
+        for i, piece in enumerate(PIECES[k]):
+            if piece[1] == done:
+                block = columns(piece)
+                for to in others:
+                    pltpu.make_async_remote_copy(
+                        src_ref=src.at[to, :, block],
+                        dst_ref=dst.at[me, :, block],
+                        send_sem=send_sem.at[k, i],
+                        recv_sem=recv_sem.at[k, i],
+                        device_id={axis: to},
+                        device_id_type=MESH,
+                    ).start()
+                dst[me, :, block] = src[me, :, block]
 
     def finish(ref, sem, piece):
         rest = ref.at[pl.ds(0, ref.shape[0] - 1), :, columns(piece)]
         pltpu.make_async_copy(rest, rest, sem).wait()
 
-    def arrive(dst, k, i):
-        finish(dst, recv_sem.at[k, i], (MA_PIECES if k < 2 else ROW_PIECES)[i])
+    def arrive(dst, k, first):
+        for i, piece in enumerate(PIECES[k]):
+            if piece[0] == first:
+                finish(dst, recv_sem.at[k, i], piece)
 
     def sent(src, k):
-        for i, piece in enumerate(MA_PIECES if k < 2 else ROW_PIECES):
+        for i, piece in enumerate(PIECES[k]):
             finish(src, send_sem.at[k, i], piece)
 
-    def swap16(parts):
-        parts = list(parts)
+    def by_holder(parts):
+        parts = [pltpu.roll(v, i, 1) if i else v for i, v in enumerate(parts)]
         for k in (1, 2, 4, 8):
-            low = (lane128 & k) == 0
-            for i in range(16):
-                if i & k == 0:
-                    a, b = parts[i], parts[i + k]
-                    parts[i] = jnp.where(low, a, pltpu.roll(b, k, 1))
-                    parts[i + k] = jnp.where(low, pltpu.roll(a, 128 - k, 1), b)
+            parts = [jnp.where((lane128 & k) == 0, parts[j], parts[(j + k) % 16]) for j in range(16)]
         return parts
+
+    def by_component(parts):
+        for k in (1, 2, 4, 8):
+            parts = [jnp.where((lane128 & k) == 0, parts[i], parts[(i - k) % 16]) for i in range(16)]
+        return [pltpu.roll(v, 128 - i, 1) if i else v for i, v in enumerate(parts)]
 
     def to_degree():
         return onehot(iota((N, N), 0) == degree)
@@ -221,7 +229,7 @@
     zt[...] = jnp.zeros_like(zt)
 
     def step(n, _):
-        for i, piece in enumerate(MA_PIECES):
+        for piece in PIECES[0]:
             low, high = piece
             for m in range(4):
                 x0 = xs[m * 4:m * 4 + 2].reshape(32, N)
@@ -240,12 +248,12 @@
                         yf[q, pl.ds(part * 4 + m, 32, stride=8), :] = block
             for q in range(low, high):
                 gs[:, :, cols(q)] = yf[q].reshape(NMA, 8, 128).astype(BF16)
-            send_ma(gs, g, 0, i)
+            send(gs, g, 0, high)
         pl.when(n == 0)(prepare_longitude)
         pl.when(n == 0)(prepare_spectral)
 
-        for i, piece in enumerate(MA_PIECES):
-            arrive(g, 0, i)
+        for piece in units(PIECES[0], PIECES[1]):
+            arrive(g, 0, piece[0])
             width = (piece[1] - piece[0]) * 128
             block = columns(piece)
             grids = [g[:, :, cols(q)].astype(F32).reshape(256, 128) for q in range(*piece)]
@@ -261,11 +269,11 @@
                 total = total + jnp.sum(value, axis=0, keepdims=True)
             out_z[:, block] = jnp.broadcast_to(total * (1.0 / NPHI), (8, width))
             ms[:, :, block] = dot(bt[...], force[:, block]).reshape(NMA, 8, width).astype(BF16)
-            send_ma(ms, h, 1, i)
+            send(ms, h, 1, piece[1])
         pl.when(n == 0)(prepare_weighted)
 
-        for i, piece in enumerate(MA_PIECES):
-            arrive(h, 1, i)
+        for i, piece in enumerate(PIECES[1]):
+            arrive(h, 1, piece[0])
             for q in range(*piece):
                 yf[q] = h[:, :, cols(q)].astype(F32).reshape(256, 128)
                 for part in range(2):
@@ -282,33 +290,33 @@
                 late = slice(piece[1] * 512, 1536)
                 back[...] = dot(zt[:, early], wp[early, :])
         sent(gs, 0)
-        for i, piece in enumerate(ROW_PIECES):
+        for piece in PIECES[2]:
             block = columns(piece)
             width = (piece[1] - piece[0]) * 128
             term = (0.25 * (back[:, block] + dot(zt[:, late], wp[late, block]))).astype(BF16).astype(F32)
             total = (spec[:, :, block].reshape(256, width) + term).astype(BF16).astype(F32)
             for q in range(*piece):
                 parts = [total[j * 16:j * 16 + 16, cols(q - piece[0])] for j in range(16)]
-                for j, part in enumerate(swap16(parts)):
+                for j, part in enumerate(by_holder(parts)):
                     rs[j, :, cols(q)] = part.astype(BF16)
-            send_row(rs, c, 2, i)
+            send(rs, c, 2, piece[1])
         sent(ms, 1)
         pl.when(n == 0)(loads[10].wait)
 
-        for i, piece in enumerate(ROW_PIECES):
-            arrive(c, 2, i)
+        for piece in units(PIECES[2], PIECES[3]):
+            arrive(c, 2, piece[0])
             for q in range(*piece):
                 right = c[:, :, cols(q)].reshape(256, 128)
                 solved = dot(inv[q * 8], right)
                 for j in range(1, 8):
-                    solved = jnp.where((lane128 >> 4) == j, dot(inv[q * 8 + j], right), solved)
+                    solved = jnp.where((((lane128 + row) & 127) >> 4) == j, dot(inv[q * 8 + j], right), solved)
                 us[:, :, cols(q)] = solved.astype(BF16).reshape(NROW, 16, 128)
-            send_row(us, s, 3, i)
+            send(us, s, 3, piece[1])
         sent(rs, 2)
-        for i, piece in enumerate(ROW_PIECES):
-            arrive(s, 3, i)
+        for piece in PIECES[3]:
+            arrive(s, 3, piece[0])
             for q in range(*piece):
-                for j, part in enumerate(swap16([s[j, :, cols(q)].astype(F32) for j in range(16)])):
+                for j, part in enumerate(by_component([s[j, :, cols(q)].astype(F32) for j in range(16)])):
                     spec[j, :, cols(q)] = part
                     xs[j, :, cols(q)] = part.astype(BF16)
         sent(us, 3)
@@ -318,7 +326,7 @@
 
 
 def unload_kernel(xs, z, out_a, out_b, out_z):
-    from_degree = onehot((iota((N, N), 0) & 15) * 24 + (iota((N, N), 0) >> 4) == iota((N, N), 1))
+    from_degree = onehot(degree_of(iota((N, N), 0)) == iota((N, N), 1))
     result = dot(xs[...].reshape(256, N), from_degree)
     for m in range(4):
         for part in range(2):

time: 105 us -> 103 us (0.981)
  Pallas kernels: 104 us -> 102 us
    pallas_call x1, Pallas kernels: 102 us -> 100 us  [shards(): pl.pallas_call(kernel, out_shape=(jax.ShapeDtypeStruct((16, 16, N), BF16)...]
where the time goes in v3:
time: 103 us
  Pallas kernels  102 us (99%)
    pallas_call x1, Pallas kernels, shards(): pl.pallas_call(kernel, out_shape=(jax.ShapeDtypeStruct((16, 16, N), BF16)...  100 us

profile of v3, /device:TPU:1, one launch (start us, length us, event | category | flops | bytes accessed | tf_op | source)
XLA Modules:
  0.0 102.8 jit_solution(16265287349063130051)
XLA Ops:
  0.6 100.1 %shell_steps.1 = (bf16[16,16,384]{2,1,0:T(8,128)(2,1)}, f32[8,384]{1,0:T(8,128)}) custom-call(f32[16,2,4,384]{3,2,1,0:T(4,128)} %fa_hbm.1, f32[16,2,4,384]{3,2,1,0:T(4,128)} %fb_hbm.1, s32[128]{0:T(128)} %ids_hbm.1, s32[384]{0:T(512)} %theta_hbm.1, bf16[4,384,384]{2,1,0:T(8,128)(2,1)} %leg_hbm.1, f32[384]{0:T(512)} %qw_hbm.1, f32[384]{0:T(512)} %colat_hbm.1, ...), custom_call_target="tpu_custom_call" | custom-call | tf_op jit(solution)/shard_map/shell_steps/pallas_call | solution.py:346
  100.8 2.0 %unload.1 = (f32[16,2,4,384]{3,2,1,0:T(4,128)}, f32[16,2,4,384]{3,2,1,0:T(4,128)}, f32[16,12]{1,0:T(8,128)}) custom-call(bf16[16,16,384]{2,1,0:T(8,128)(2,1)} %get-tuple-element.5.xs, f32[8,384]{1,0:T(8,128)} %get-tuple-element.6.z), custom_call_target="tpu_custom_call" | custom-call | tf_op jit(solution)/shard_map/unload/pallas_call | solution.py:398

commit v4 on v3

--- a/solution.py
+++ b/solution.py
@@ -163,7 +163,6 @@
     def prepare_spectral():
         hot = to_degree()
         for m in range(4):
-            legp[m] = dot(legp[m], hot).astype(BF16)
             alive = lane >= ids_s[ma * 4 + m]
             for part in range(2):
                 for f, field in ((0, fa), (1, fb)):
@@ -171,6 +170,11 @@
                     hi = piece.astype(BF16)
                     lo = (piece - hi.astype(F32)).astype(BF16)
                     spec[m * 4 + part * 2 + f] = dot(hi, hot) + dot(lo, hot)
+
+    def prepare_synthesis():
+        hot = to_degree()
+        for m in range(4):
+            legp[m] = dot(legp[m], hot).astype(BF16)
 
     def prepare_longitude():
         for load in loads[5:9]:
@@ -301,6 +305,7 @@
                     rs[j, :, cols(q)] = part.astype(BF16)
             send(rs, c, 2, piece[1])
         sent(ms, 1)
+        pl.when(n == 0)(prepare_synthesis)
         pl.when(n == 0)(loads[10].wait)
 
         for piece in units(PIECES[2], PIECES[3]):

time: 103 us -> 103 us (level)
  no operation moved by 1% of the time
where the time goes in v4:
time: 103 us; the launch traced here: 102 us
  Pallas kernels  102 us (99%)
    pallas_call x1, Pallas kernels, shards(): pl.pallas_call(kernel, out_shape=(jax.ShapeDtypeStruct((16, 16, N), BF16)...  99.7 us

profile of v4, /device:TPU:1, one launch (start us, length us, event | category | flops | bytes accessed | tf_op | source)
XLA Modules:
  0.0 102.4 jit_solution(16613566399577712424)
XLA Ops:
  0.6 99.7 %shell_steps.1 = (bf16[16,16,384]{2,1,0:T(8,128)(2,1)}, f32[8,384]{1,0:T(8,128)}) custom-call(f32[16,2,4,384]{3,2,1,0:T(4,128)} %fa_hbm.1, f32[16,2,4,384]{3,2,1,0:T(4,128)} %fb_hbm.1, s32[128]{0:T(128)} %ids_hbm.1, s32[384]{0:T(512)} %theta_hbm.1, bf16[4,384,384]{2,1,0:T(8,128)(2,1)} %leg_hbm.1, f32[384]{0:T(512)} %qw_hbm.1, f32[384]{0:T(512)} %colat_hbm.1, ...), custom_call_target="tpu_custom_call" | custom-call | tf_op jit(solution)/shard_map/shell_steps/pallas_call | solution.py:351
  100.4 2.0 %unload.1 = (f32[16,2,4,384]{3,2,1,0:T(4,128)}, f32[16,2,4,384]{3,2,1,0:T(4,128)}, f32[16,12]{1,0:T(8,128)}) custom-call(bf16[16,16,384]{2,1,0:T(8,128)(2,1)} %get-tuple-element.5.xs, f32[8,384]{1,0:T(8,128)} %get-tuple-element.6.z), custom_call_target="tpu_custom_call" | custom-call | tf_op jit(solution)/shard_map/unload/pallas_call | solution.py:403
